TPU v7x, 32 devices: a whole 2x2x4 slice. The times are simulated.
32 devices in a mesh: groups: 2 (over y), gr: 4 (over z), gc: 4 (over x, core).
Axes of the slice: x: 2, y: 2, z: 4, core: 2. Of those that a mesh axis runs over, the one named last changes fastest.
Arguments:
- embeddings: bfloat16 [3072, 256], P(('groups', 'gr', 'gc')), parts along dimension 0, may hold values from -6 to 6
- thresholds: bfloat16 [3072], P(('groups', 'gr', 'gc')), parts along dimension 0, may hold values from 0.119628906 to 0.359375
- valid: int32 [3072], P(('groups', 'gr', 'gc')), parts along dimension 0, may hold values 0 or 1
Outputs:
- row_mix: bfloat16 [3072, 256], P(('groups', 'gr', 'gc')), parts along dimension 0
- partner_mix: bfloat16 [3072, 256], P(('groups', 'gr', 'gc')), parts along dimension 0
There are 2 independent parts, one for each index of `groups`. A program takes and returns all parts, laid end to end along the dimension named above; each array names one. Nothing has to cross between parts.
All inputs are finite; a program needn't handle non-finite values. No bound on the sum of `valid` on one device may be relied on, other than what follows from the above.
Results may differ from a plain program's by a relative error of at most 0.0064.
Values may be sent and summed in bfloat16 or wider, within the bound.
A program may use at most 64 MiB of HBM per device.

v0:
```python
import jax
import jax.numpy as jnp
from jax import lax
from jax.sharding import PartitionSpec as P

sharpness = 40.0


def weigh(rows_unit, rows_limit, rows_member, part_unit, part_member):
    scores = lax.dot_general(
        rows_unit, part_unit, (((1,), (1,)), ((), ())), preferred_element_type=jnp.float32
    )
    return (
        jax.nn.sigmoid(sharpness * (scores - rows_limit[:, None]))
        * rows_member[:, None]
        * part_member[None, :]
    )


def per_device(embeddings, thresholds, valid):
    emb = embeddings.astype(jnp.float32)
    unit = (emb * lax.rsqrt(jnp.sum(emb * emb, axis=1, keepdims=True) + 1e-06)).astype(jnp.bfloat16)
    member_low = valid.astype(jnp.bfloat16)
    rows_unit, rows_limit_low, rows_member_low = (
        lax.all_gather(unit, "gc", axis=0, tiled=True),
        lax.all_gather(thresholds, "gc", axis=0, tiled=True),
        lax.all_gather(member_low, "gc", axis=0, tiled=True),
    )
    part_unit, part_member_low = (
        lax.all_gather(unit, "gr", axis=0, tiled=True),
        lax.all_gather(member_low, "gr", axis=0, tiled=True),
    )
    rows_limit = rows_limit_low.astype(jnp.float32)
    rows_member = rows_member_low.astype(jnp.float32)
    part_member = part_member_low.astype(jnp.float32)
    row_count = rows_unit.shape[0]
    part_count = part_unit.shape[0]
    width = embeddings.shape[1]
    scale = width**0.5
    block = 512 if part_count % 512 == 0 else part_count
    steps_count = part_count // block
    unit_blocks = part_unit.reshape(steps_count, block, width)
    member_blocks = part_member.reshape(steps_count, block)

    def step(carry, piece):
        row_sum, row_total = carry
        piece_unit, piece_member = piece
        weight = weigh(rows_unit, rows_limit, rows_member, piece_unit, piece_member)
        weight_low = weight.astype(jnp.bfloat16)
        row_sum = row_sum + jnp.dot(weight_low, piece_unit, preferred_element_type=jnp.float32)
        row_total = row_total + jnp.sum(weight, axis=1)
        back_sum = lax.dot_general(
            weight_low, rows_unit, (((0,), (0,)), ((), ())), preferred_element_type=jnp.float32
        )
        return ((row_sum, row_total), (back_sum, jnp.sum(weight, axis=0)))

    start = (jnp.zeros((row_count, width), jnp.float32), jnp.zeros((row_count,), jnp.float32))
    (row_sum, row_total), (back_blocks, back_totals) = lax.scan(
        step, start, (unit_blocks, member_blocks)
    )
    partner_sum = back_blocks.reshape(part_count, width)
    partner_total = back_totals.reshape(part_count)
    own_sum, own_total = (
        lax.psum_scatter(row_sum, "gc", scatter_dimension=0, tiled=True),
        lax.psum_scatter(row_total, "gc", scatter_dimension=0, tiled=True),
    )
    mine_sum, mine_total = (
        lax.psum_scatter(partner_sum, "gr", scatter_dimension=0, tiled=True),
        lax.psum_scatter(partner_total, "gr", scatter_dimension=0, tiled=True),
    )
    row_mix = (scale * own_sum / (1.0 + own_total[:, None])).astype(jnp.bfloat16)
    partner_mix = (scale * mine_sum / (1.0 + mine_total[:, None])).astype(jnp.bfloat16)
    return (row_mix, partner_mix)


def solution(mesh):
    return jax.shard_map(
        per_device,
        mesh=mesh,
        in_specs=(
            P(("groups", "gr", "gc"), None),
            P(("groups", "gr", "gc")),
            P(("groups", "gr", "gc")),
        ),
        out_specs=(P(("groups", "gr", "gc"), None), P(("groups", "gr", "gc"), None)),
        check_vma=False,
    )
```

profile of v0, /device:TPU:1, one launch (start us, length us, event | category | flops | bytes accessed | tf_op | source)
XLA Modules:
  0.0 101.5 jit_solution(12980932226297836933)
XLA Ops:
  7.2 0.9 fusion.11
  8.2 0.1 fusion.12
  8.3 6.7 %all_gather.15 = bf16[384,256]{1,0:T(8,128)(2,1)S(1)} all-gather(bf16[96,256]{1,0:T(8,128)(2,1)S(1)} %fusion.12), channel_id=1, replica_groups=mesh['groups'=2,'gr'=4,'gc'=4] {'gc'}, dimensions={0}, use_global_device_ids=true | all-gather | bytes 245760 | tf_op jit(solution)/shard_map/all_gather | solution.py:25
  15.0 11.9 %all_gather.16 = bf16[384,256]{1,0:T(8,128)(2,1)S(1)} all-gather(bf16[96,256]{1,0:T(8,128)(2,1)S(1)} %fusion.12), channel_id=1, replica_groups=mesh['groups'=2,'gr'=4,'gc'=4] {'gr'}, dimensions={0}, use_global_device_ids=true | all-gather | bytes 245760 | tf_op jit(solution)/shard_map/all_gather | solution.py:30
  27.0 0.6 copy-done.1
  27.6 0.7 fusion.14
  29.0 0.2 dynamic-update-slice.1
  29.2 0.7 copy-done.4
  29.9 0.2 dynamic-update-slice
  30.1 7.4 %all-reduce.5 = (bf16[384]{0:T(512)(128)(2,1)S(1)}, bf16[384]{0:T(512)(128)(2,1)S(1)}) all-reduce(bf16[384]{0:T(512)(128)(2,1)S(1)} %dynamic-update-slice.1, bf16[384]{0:T(512)(128)(2,1)S(1)} %dynamic-update-slice), channel_id=1, replica_groups=mesh['groups'=2,'gr'=4,'gc'=4] {'gc'}, use_global_device_ids=true, to_apply=%add.1 | all-reduce | flops 768 | bytes 3072
  38.1 0.2 dynamic-update-slice.2
  38.4 10.1 %all-reduce.2 = bf16[384]{0:T(512)(128)(2,1)S(1)} all-reduce(bf16[384]{0:T(512)(128)(2,1)S(1)} %dynamic-update-slice.2), channel_id=1, replica_groups=mesh['groups'=2,'gr'=4,'gc'=4] {'gr'}, use_global_device_ids=true, to_apply=%add.2 | all-reduce | flops 384 | bytes 1536
  48.5 0.5 fusion.13
  48.9 1.1 %fusion.7 = f32[384,256]{1,0:T(8,128)} fusion(bf16[384,256]{1,0:T(8,128)(2,1)S(1)} %all_gather.15, bf16[384,384]{1,0:T(8,128)(2,1)S(1)} %get-tuple-element.40), kind=kOutput, calls=%fused_computation.8 | convolution fusion | flops 75497472 | bytes 884736 | tf_op jit(solution)/shard_map/while/body/eval_jaxpr/dot_general | solution.py:52
  50.0 0.0 reduce-scatter.3.cloned.1.call-start
  50.1 1.0 fusion.9
  52.4 6.7 %all-reduce.4 = f32[384]{0:T(512)S(1)} all-reduce(f32[384]{0:T(512)S(1)} %get-tuple-element.22), channel_id=5, replica_groups=mesh['groups'=2,'gr'=4,'gc'=4] {'gr'}, use_global_device_ids=true, to_apply=%region_6.7.clone | all-reduce | flops 384 | bytes 3072
  59.1 9.5 %all-reduce.3 = f32[384]{0:T(512)S(1)} all-reduce(f32[384]{0:T(512)S(1)} %get-tuple-element.23), channel_id=3, replica_groups=mesh['groups'=2,'gr'=4,'gc'=4] {'gc'}, use_global_device_ids=true, to_apply=%region_3.4.clone | all-reduce | flops 384 | bytes 3072
  68.6 0.1 dynamic-slice_add_fusion
  68.7 0.1 dynamic-slice_add_fusion.1
  68.8 0.9 reduce-scatter.5.cloned.1.call-done
  69.6 1.6 %divide_convert_fusion = bf16[96,256]{1,0:T(8,128)(2,1)} fusion(f32[96,256]{1,0:T(8,128)} %reduce-scatter.5.cloned.1.call-done, f32[96]{0:T(128)S(1)} %dynamic-slice_add_fusion), kind=kLoop, calls=%fused_computation.16 | loop fusion | flops 73728 | bytes 147840 | tf_op jit(solution)/shard_map/convert_element_type | solution.py:72
  71.2 21.8 %reduce-scatter.3.cloned.1.call-done = f32[96,256]{1,0:T(8,128)} async-done(((f32[384,256]{1,0:T(8,128)}), f32[96,256]{1,0:T(8,128)}) %reduce-scatter.3.cloned.1.call-update) | async-done | bytes 98320 | tf_op jit(solution)/shard_map/reduce_scatter | solution.py:64
  93.0 1.6 %divide_convert_fusion.1 = bf16[96,256]{1,0:T(8,128)(2,1)} fusion(f32[96,256]{1,0:T(8,128)} %reduce-scatter.3.cloned.1.call-done, f32[96]{0:T(128)S(1)} %dynamic-slice_add_fusion.1), kind=kLoop, calls=%fused_computation.17 | loop fusion | flops 73728 | bytes 147840 | tf_op jit(solution)/shard_map/convert_element_type | solution.py:71
  (19 shorter events, 0.1 us)
Async XLA Ops:
  7.2 1.0 copy-start
  7.2 62.5 %reduce-scatter.5.cloned.1.call-start = ((), (), s32[]{:S(2)}) async-start(), calls=%async_computation.3 | async-start | bytes 491520 | tf_op jit(solution)/shard_map/reduce_scatter | solution.py:68
  15.0 11.9 %copy-start.3 = (s32[96]{0:T(128)S(1)}, s32[96]{0:T(128)}, u32[]{:S(2)}) copy-start(s32[96]{0:T(128)} %param.5) | copy-start | bytes 1156
  26.9 0.7 copy-start.1
  26.9 0.7 copy-start.2
  29.2 0.7 copy-start.4
  50.0 43.0 %reduce-scatter.3.cloned.1.call-start = ((), (), s32[]{:S(2)}) async-start(), calls=%async_computation.2 | async-start | bytes 491520 | tf_op jit(solution)/shard_map/reduce_scatter | solution.py:64
Sparse Core Ops, SparseCore 0:
  50.1 19.4 reduce-scatter.4
  72.3 20.7 reduce-scatter.2
where the time goes:
time: 102 us; the launch traced here: 101 us
  blocking collectives  52.3 us (51%)
  waiting for transfers between devices  22.7 us (22%)
  between operations  16.8 us (16%)
  other arithmetic  4.36 us (4%)
  local copies, waits for them, and re-layouts  2.67 us (3%)
  matrix products  2.52 us (2%)
    unnamed x4, blocking collectives  33.7 us
    reduce_scatter x1, waiting for transfers between devices, per_device(): lax.psum_scatter(row_sum, 'gc', scatter_dimension=0, tiled=True)  21.8 us
    all_gather x1, blocking collectives, per_device(): lax.all_gather(unit, 'gr', axis=0, tiled=True)  11.9 us
    all_gather x1, blocking collectives, per_device(): lax.all_gather(unit, 'gc', axis=0, tiled=True)  6.73 us
    unnamed x17, local copies, waits for them, and re-layouts  2.67 us
  transfers between devices with their start and end apart: 2, of which 2 were waited for; matrix products, arithmetic and copies ran while one was open for 3% of the time, Pallas kernels for 0%

commit v1 on v0

v1 whole, which is shorter than its diff:
```python
import functools

import jax
import jax.numpy as jnp
from jax import lax
from jax.experimental import pallas as pl
from jax.experimental.pallas import tpu as pltpu
from jax.sharding import PartitionSpec as P

sharpness = 40.0
LANES = 128
EXTRA = 16
FAR = 1e9
MESH = pl.DeviceIdType.MESH


def kernel(n_r, n_c, emb_ref, lim_ref, val_ref, row_ref, part_ref, buf, send_z, send_x, send_c, recv):
    rows, width = emb_ref.shape
    cols = width // LANES
    n_x = n_c // 2
    z = lax.axis_index("gr")
    g = lax.axis_index("gc")
    core = lax.rem(g, 2)
    xx = g // 2
    twin = g + 1 - 2 * core
    loop = functools.partial(lax.fori_loop, unroll=n_r <= 4)

    def z_peer(k):
        return lax.rem(z + k, n_r)

    def x_peer(k):
        return lax.rem(xx + k, n_x) * 2 + core

    def to(z_to, g_to):
        return {"gr": z_to, "gc": g_to}

    barrier = pltpu.get_barrier_semaphore()

    def greet(z_to, g_to):
        pl.semaphore_signal(barrier, inc=1, device_id=to(z_to, g_to), device_id_type=MESH)

    def each(first, last, do):
        def body(k, carry):
            do(k)
            return carry

        loop(first, last, body, 0)

    each(1, n_r, lambda k: greet(z_peer(k), g))
    each(1, n_x, lambda k: greet(z, x_peer(k)))
    greet(z, twin)

    emb = emb_ref[...].astype(jnp.float32)
    unit = (emb * lax.rsqrt(jnp.sum(emb * emb, axis=1, keepdims=True) + 1e-06)).astype(jnp.bfloat16)
    for c in range(cols):
        buf[z, g, c * rows:(c + 1) * rows, :] = unit[:, c * LANES:(c + 1) * LANES]
    lim_row = lim_ref[...].astype(jnp.float32).reshape(1, rows)
    val_row = val_ref[...].reshape(1, rows)
    far_row = jnp.where(val_row > 0, lim_row, FAR)
    far_pad = jnp.concatenate([far_row, jnp.full((1, LANES - rows), FAR, jnp.float32)], axis=1)
    buf[z, g, cols * rows:, :] = jnp.broadcast_to(far_pad, (EXTRA, LANES)).astype(jnp.bfloat16)

    pl.semaphore_wait(barrier, n_r + n_x - 1)

    def copy(z_of, g_of, sem, z_to, g_to):
        return pltpu.make_async_remote_copy(
            src_ref=buf.at[z_of, g_of],
            dst_ref=buf.at[z_of, g_of],
            send_sem=sem,
            recv_sem=recv.at[z_of, g_of],
            device_id=to(z_to, g_to),
            device_id_type=MESH,
        )

    def copy_z(k):
        return copy(z, g, send_z.at[k - 1], z_peer(k), g)

    def copy_x(p, k):
        return copy(z_peer(p), g, send_x.at[p, k - 1], z, x_peer(k))

    def copy_c(p, k):
        return copy(z_peer(p), x_peer(k), send_c.at[p, k], z, twin)

    def arrived(z_of, g_of):
        copy(z_of, g_of, send_z.at[0], z, twin).wait_recv()

    each(1, n_r, lambda k: copy_z(k).start())
    each(1, n_x, lambda k: copy_x(0, k).start())
    copy_c(0, 0).start()

    eye = lax.broadcasted_iota(jnp.int32, (rows, rows), 0) == lax.broadcasted_iota(jnp.int32, (rows, rows), 1)
    lim_col = jnp.sum(jnp.where(eye, lim_row, 0.0), axis=1, keepdims=True)
    val_col = jnp.sum(jnp.where(eye, val_row.astype(jnp.float32), 0.0), axis=1, keepdims=True)

    def pass_on(p):
        arrived(z_peer(p), g)
        each(1, n_x, lambda k: copy_x(p, k).start())
        copy_c(p, 0).start()

    def hand_over(p):
        def one(k):
            arrived(z_peer(p), x_peer(k))
            copy_c(p, k).start()

        each(1, n_x, one)

    def collect(p):
        def one(k):
            arrived(z_peer(p), lax.rem(xx + k, n_x) * 2 + 1 - core)

        each(0, n_x, one)

    def add(p, carry):
        sums, row_total, part_total = carry
        at = z_peer(p)
        others = jnp.concatenate(
            [buf[at, :, c * rows:(c + 1) * rows, :].reshape(n_c * rows, LANES) for c in range(cols)], axis=1
        )
        scores = lax.dot_general(
            unit, others, (((1,), (1,)), ((), ())), preferred_element_type=jnp.float32
        )
        far = jnp.concatenate(
            [buf[at, j, cols * rows:, :].astype(jnp.float32)[:1, :rows] for j in range(n_c)], axis=1
        )
        gone = far > 0.5 * FAR
        by_row = jnp.where(gone, 0.0, 0.5 + 0.5 * jnp.tanh(0.5 * sharpness * (scores - lim_col)))
        by_part = 0.5 + 0.5 * jnp.tanh(0.5 * sharpness * (scores - far))
        low = jnp.concatenate([by_row.astype(jnp.bfloat16), by_part.astype(jnp.bfloat16)], axis=0)
        sums = sums + jnp.dot(low, others, preferred_element_type=jnp.float32)
        row_total = row_total + jnp.sum(by_row, axis=1, keepdims=True)
        part_total = part_total + jnp.sum(by_part, axis=1, keepdims=True)
        return sums, row_total, part_total

    carry = (
        jnp.zeros((2 * rows, width), jnp.float32),
        jnp.zeros((rows, 1), jnp.float32),
        jnp.zeros((rows, 1), jnp.float32),
    )
    hand_over(0)

    def step(p, carry):
        pass_on(p)
        collect(p - 1)
        carry = add(p - 1, carry)
        hand_over(p)
        return carry

    carry = loop(1, n_r, step, carry)
    collect(n_r - 1)
    sums, row_total, part_total = add(n_r - 1, carry)

    scale = width**0.5 * val_col
    row_ref[...] = (sums[:rows] * (scale / (1.0 + row_total))).astype(jnp.bfloat16)
    part_ref[...] = (sums[rows:] * (scale / (1.0 + part_total))).astype(jnp.bfloat16)

    each(1, n_r, lambda k: copy_z(k).wait_send())

    def sent(p):
        each(1, n_x, lambda k: copy_x(p, k).wait_send())
        each(0, n_x, lambda k: copy_c(p, k).wait_send())

    each(0, n_r, sent)


def per_device(n_r, n_c, embeddings, thresholds, valid):
    rows, width = embeddings.shape
    vmem = pl.BlockSpec(memory_space=pltpu.VMEM)
    out = jax.ShapeDtypeStruct((rows, width), jnp.bfloat16)
    shard = (width // LANES) * rows + EXTRA
    return pl.pallas_call(
        functools.partial(kernel, n_r, n_c),
        out_shape=(out, out),
        in_specs=[vmem] * 3,
        out_specs=(vmem, vmem),
        scratch_shapes=[
            pltpu.VMEM((n_r, n_c, shard, LANES), jnp.bfloat16),
            pltpu.SemaphoreType.DMA((n_r - 1,)),
            pltpu.SemaphoreType.DMA((n_r, n_c // 2 - 1)),
            pltpu.SemaphoreType.DMA((n_r, n_c // 2)),
            pltpu.SemaphoreType.DMA((n_r, n_c)),
        ],
        compiler_params=pltpu.CompilerParams(
            collective_id=0, has_side_effects=True, vmem_limit_bytes=48 * 1024 * 1024
        ),
    )(embeddings, thresholds.reshape(1, rows), valid.reshape(1, rows))


def solution(mesh):
    return jax.shard_map(
        functools.partial(per_device, mesh.shape["gr"], mesh.shape["gc"]),
        mesh=mesh,
        in_specs=(
            P(("groups", "gr", "gc"), None),
            P(("groups", "gr", "gc")),
            P(("groups", "gr", "gc")),
        ),
        out_specs=(P(("groups", "gr", "gc"), None), P(("groups", "gr", "gc"), None)),
        check_vma=False,
    )
```

time: 102 us -> 24.3 us (0.24)
  blocking collectives: 52.3 us -> 0 us
  waiting for transfers between devices: 22.7 us -> 0 us
  Pallas kernels: 0 us -> 20.8 us
  between operations: 16.8 us -> 0.66 us
  other arithmetic: 4.36 us -> 0 us
  matrix products: 2.52 us -> 0 us
    unnamed x4 -> x0, blocking collectives: 33.7 us -> none
    reduce_scatter x2 -> x0, waiting for transfers between devices: 22.7 us -> none  [the longest x1 21.8 us: per_device(): lax.psum_scatter(row_sum, 'gc', scatter_dimension=0, tiled=True)]
    pallas_call x0 -> x1, Pallas kernels: none -> 20.8 us  [per_device(): pl.pallas_call(functools.partial(kernel, n_r, n_c), out_shape=(out, out),...]
    all_gather x2 -> x0, blocking collectives: 18.7 us -> none  [the longest x1 11.9 us: per_device(): lax.all_gather(unit, 'gr', axis=0, tiled=True)]
    convert_element_type x7 -> x0, other arithmetic: 3.3 us -> none  [the longest x1 1.6 us: per_device(): (scale * mine_sum / (1.0 + mine_total[:, None])).astype(jnp.bfloat16)]
    dot_general x3 -> x0, matrix products: 2.52 us -> none  [the longest x1 1.06 us: step(): lax.dot_general(weight_low, rows_unit, (((0,), (0,)), ((), ())), preferre...]
    unnamed x17 -> x8, local copies, waits for them, and re-layouts: 2.67 us -> 2.7 us
  transfers between devices with their start and end apart: 2 -> 0, of which waited for: 2 -> 0; matrix products, arithmetic and copies ran while one was open for 3% -> 0% of each run, Pallas kernels for 0% -> 0%
where the time goes in v1:
time: 24.3 us; the launch traced here: 24.2 us
  Pallas kernels  20.8 us (86%)
  local copies, waits for them, and re-layouts  2.7 us (11%)
  between operations  0.66 us (3%)
    pallas_call x1, Pallas kernels, per_device(): pl.pallas_call(functools.partial(kernel, n_r, n_c), out_shape=(out, out),...  20.8 us
    unnamed x8, local copies, waits for them, and re-layouts  2.7 us

profile of v1, /device:TPU:1, one launch (start us, length us, event | category | flops | bytes accessed | tf_op | source)
XLA Modules:
  0.0 24.2 jit_solution(14957945183522606367)
XLA Ops:
  0.6 0.0 copy-start.1
  0.6 0.0 copy-start.2
  0.6 0.6 %copy-done.1 = bf16[96]{0:T(256)(128)(2,1)S(1)} copy-done((bf16[96]{0:T(256)(128)(2,1)S(1)}, bf16[96]{0:T(256)(128)(2,1)}, u32[]{:S(2)}) %copy-start.1) | copy-done | bytes 216
  1.3 0.0 copy-done.2
  1.3 0.0 copy-start
  1.3 0.8 %copy-done = bf16[96,256]{1,0:T(8,128)(2,1)S(1)} copy-done((bf16[96,256]{1,0:T(8,128)(2,1)S(1)}, bf16[96,256]{1,0:T(8,128)(2,1)}, u32[]{:S(2)}) %copy-start) | copy-done | bytes 49176
  2.1 20.8 %shard_map.50 = (bf16[96,256]{1,0:T(8,128)(2,1)S(1)}, bf16[96,256]{1,0:T(8,128)(2,1)S(1)}) custom-call(bf16[96,256]{1,0:T(8,128)(2,1)S(1)} %copy-done, bf16[1,96]{1,0:T(2,128)(2,1)S(1)} %bitcast.2, s32[1,96]{1,0:T(1,128)S(1)} %bitcast.3), custom_call_target="tpu_custom_call" | custom-call | tf_op jit(solution)/shard_map/pallas_call | solution.py:170
  22.9 0.6 %copy.7 = bf16[96,256]{1,0:T(8,128)(2,1)} copy(bf16[96,256]{1,0:T(8,128)(2,1)S(1)} %get-tuple-element.4) | data formatting | bytes 98304
  23.5 0.6 %copy.8 = bf16[96,256]{1,0:T(8,128)(2,1)} copy(bf16[96,256]{1,0:T(8,128)(2,1)S(1)} %get-tuple-element.5) | data formatting | bytes 98304
Async XLA Ops:
  0.6 0.7 %copy-start.1 = (bf16[96]{0:T(256)(128)(2,1)S(1)}, bf16[96]{0:T(256)(128)(2,1)}, u32[]{:S(2)}) copy-start(bf16[96]{0:T(256)(128)(2,1)} %param.4) | copy-start | bytes 580
  0.6 0.7 %copy-start.2 = (s32[96]{0:T(128)S(1)}, s32[96]{0:T(128)}, u32[]{:S(2)}) copy-start(s32[96]{0:T(128)} %param.5) | copy-start | bytes 1156
  1.3 0.8 %copy-start = (bf16[96,256]{1,0:T(8,128)(2,1)S(1)}, bf16[96,256]{1,0:T(8,128)(2,1)}, u32[]{:S(2)}) copy-start(bf16[96,256]{1,0:T(8,128)(2,1)} %emb_ref.1) | copy-start | bytes 147460

commit v2 on v1

v2 whole, which is shorter than its diff:
```python
import functools

import jax
import jax.numpy as jnp
from jax import lax
from jax.experimental import pallas as pl
from jax.experimental.pallas import tpu as pltpu
from jax.sharding import PartitionSpec as P

sharpness = 40.0
LANES = 128
EXTRA = 16
FAR = 1e9
MESH = pl.DeviceIdType.MESH


def kernel(
    n_r, n_x, emb_hbm, lim_hbm, val_hbm, row_ref, part_ref,
    buf, emb_ref, lim_ref, val_ref, send, send_c, recv, load,
):
    rows, width = emb_ref.shape
    cols = width // LANES
    z = lax.axis_index("gr")
    g = lax.axis_index("gc")
    core = lax.rem(g, 2)
    x = g // 2
    few = n_r * n_x <= 8

    loads = [
        pltpu.make_async_copy(src, dst, load.at[i])
        for i, (src, dst) in enumerate(((emb_hbm, emb_ref), (lim_hbm, lim_ref), (val_hbm, val_ref)))
    ]
    for one in loads:
        one.start()

    def plane(p):
        return lax.rem(z + p, n_r)

    def column(k):
        return lax.rem(x + k, n_x)

    def device(z_to, x_to, core_to):
        return {"gr": z_to, "gc": x_to * 2 + core_to}

    def each(first, last, do):
        def body(i, carry):
            do(lax.rem(i, n_r), i // n_r)
            return carry

        if few:
            for i in range(first, last):
                do(i % n_r, i // n_r)
        else:
            lax.fori_loop(first, last, body, 0)

    barrier = pltpu.get_barrier_semaphore()

    def greet(z_to, x_to, core_to):
        pl.semaphore_signal(barrier, inc=1, device_id=device(z_to, x_to, core_to), device_id_type=MESH)

    each(1, n_r * n_x, lambda p, k: greet(plane(p), column(k), core))
    greet(z, x, 1 - core)

    for one in loads:
        one.wait()
    emb = emb_ref[...].astype(jnp.float32)
    unit = (emb * lax.rsqrt(jnp.sum(emb * emb, axis=1, keepdims=True) + 1e-06)).astype(jnp.bfloat16)
    for c in range(cols):
        buf[z, x, core, c * rows:(c + 1) * rows, :] = unit[:, c * LANES:(c + 1) * LANES]
    lim_row = lim_ref[...].astype(jnp.float32)
    val_row = val_ref[...]
    far_row = jnp.where(val_row > 0, lim_row, FAR)
    far_pad = jnp.concatenate([far_row, jnp.full((1, LANES - rows), FAR, jnp.float32)], axis=1)
    buf[z, x, core, cols * rows:, :] = jnp.broadcast_to(far_pad, (EXTRA, LANES)).astype(jnp.bfloat16)

    eye = lax.broadcasted_iota(jnp.int32, (rows, rows), 0) == lax.broadcasted_iota(jnp.int32, (rows, rows), 1)
    lim_col = jnp.sum(jnp.where(eye, lim_row, 0.0), axis=1, keepdims=True)
    val_col = jnp.sum(jnp.where(eye, val_row.astype(jnp.float32), 0.0), axis=1, keepdims=True)

    pl.semaphore_wait(barrier, n_r * n_x)

    def copy(z_of, x_of, core_of, sem, to):
        return pltpu.make_async_remote_copy(
            src_ref=buf.at[z_of, x_of, core_of],
            dst_ref=buf.at[z_of, x_of, core_of],
            send_sem=sem,
            recv_sem=recv.at[z_of, x_of, core_of],
            device_id=to,
            device_id_type=MESH,
        )

    def out(p, k):
        return copy(z, x, core, send.at[p, k], device(plane(p), column(k), core))

    def over(p, k):
        return copy(plane(p), column(k), core, send_c.at[p, k], device(z, x, 1 - core))

    def arrived(p, k, core_of):
        copy(plane(p), column(k), core_of, send_c.at[0, 0], device(z, x, 1 - core)).wait_recv()

    if few:
        order = [(p, k) for k in reversed(range(n_x)) for p in range(n_r) if p or k]
        for p, k in order:
            out(p, k).start()
    else:
        each(1, n_r * n_x, lambda p, k: out(p, k).start())
    over(0, 0).start()

    def pass_on(p, k):
        arrived(p, k, core)
        over(p, k).start()

    def add(planes, k, carry):
        sums, row_total, part_total = carry
        others = jnp.concatenate(
            [
                jnp.concatenate(
                    [buf[plane(p), column(k), :, c * rows:(c + 1) * rows, :].reshape(2 * rows, LANES) for p in planes],
                    axis=0,
                )
                for c in range(cols)
            ],
            axis=1,
        )
        scores = lax.dot_general(
            unit, others, (((1,), (1,)), ((), ())), preferred_element_type=jnp.float32
        )
        far = jnp.concatenate(
            [
                buf[plane(p), column(k), j, cols * rows:, :].astype(jnp.float32)[:1, :rows]
                for p in planes
                for j in range(2)
            ],
            axis=1,
        )
        gone = far > 0.5 * FAR
        by_row = jnp.where(gone, 0.0, 0.5 + 0.5 * jnp.tanh(0.5 * sharpness * (scores - lim_col)))
        by_part = 0.5 + 0.5 * jnp.tanh(0.5 * sharpness * (scores - far))
        low = jnp.concatenate([by_row.astype(jnp.bfloat16), by_part.astype(jnp.bfloat16)], axis=0)
        sums = sums + jnp.dot(low, others, preferred_element_type=jnp.float32)
        row_total = row_total + jnp.sum(by_row, axis=1, keepdims=True)
        part_total = part_total + jnp.sum(by_part, axis=1, keepdims=True)
        return sums, row_total, part_total

    carry = (
        jnp.zeros((2 * rows, width), jnp.float32),
        jnp.zeros((rows, 1), jnp.float32),
        jnp.zeros((rows, 1), jnp.float32),
    )
    if few:
        for p in range(1, n_r):
            pass_on(p, 0)
        for p in range(n_r):
            arrived(p, 0, 1 - core)
        carry = add(range(n_r), 0, carry)
        half = (n_r + 1) // 2
        for k in range(1, n_x):
            for p in range(n_r):
                pass_on(p, k)
            for planes in (range(half), range(half, n_r)):
                for p in planes:
                    arrived(p, k, 1 - core)
                carry = add(planes, k, carry)
    else:
        each(1, n_r * n_x, pass_on)
        each(0, n_r * n_x, lambda p, k: arrived(p, k, 1 - core))

        def step(i, carry):
            return add((lax.rem(i, n_r),), i // n_r, carry)

        carry = lax.fori_loop(0, n_r * n_x, step, carry)
    sums, row_total, part_total = carry

    scale = width**0.5 * val_col
    row_ref[...] = (sums[:rows] * (scale / (1.0 + row_total))).astype(jnp.bfloat16)
    part_ref[...] = (sums[rows:] * (scale / (1.0 + part_total))).astype(jnp.bfloat16)

    each(1, n_r * n_x, lambda p, k: out(p, k).wait_send())
    each(0, n_r * n_x, lambda p, k: over(p, k).wait_send())


def per_device(n_r, n_x, embeddings, thresholds, valid):
    rows, width = embeddings.shape
    hbm = pl.BlockSpec(memory_space=pltpu.HBM)
    vmem = pl.BlockSpec(memory_space=pltpu.VMEM)
    out = jax.ShapeDtypeStruct((rows, width), jnp.bfloat16)
    shard = (width // LANES) * rows + EXTRA
    return pl.pallas_call(
        functools.partial(kernel, n_r, n_x),
        out_shape=(out, out),
        in_specs=[hbm] * 3,
        out_specs=(vmem, vmem),
        scratch_shapes=[
            pltpu.VMEM((n_r, n_x, 2, shard, LANES), jnp.bfloat16),
            pltpu.VMEM((rows, width), embeddings.dtype),
            pltpu.VMEM((1, rows), thresholds.dtype),
            pltpu.VMEM((1, rows), valid.dtype),
            pltpu.SemaphoreType.DMA((n_r, n_x)),
            pltpu.SemaphoreType.DMA((n_r, n_x)),
            pltpu.SemaphoreType.DMA((n_r, n_x, 2)),
            pltpu.SemaphoreType.DMA((3,)),
        ],
        compiler_params=pltpu.CompilerParams(
            collective_id=0, has_side_effects=True, vmem_limit_bytes=48 * 1024 * 1024
        ),
    )(embeddings, thresholds.reshape(1, rows), valid.reshape(1, rows))


def solution(mesh):
    return jax.shard_map(
        functools.partial(per_device, mesh.shape["gr"], mesh.shape["gc"] // 2),
        mesh=mesh,
        in_specs=(
            P(("groups", "gr", "gc"), None),
            P(("groups", "gr", "gc")),
            P(("groups", "gr", "gc")),
        ),
        out_specs=(P(("groups", "gr", "gc"), None), P(("groups", "gr", "gc"), None)),
        check_vma=False,
    )
```

time: 24.3 us -> 22.3 us (0.918)
  the two profiles are of different devices: /device:TPU:1 before, /device:TPU:0 now
where the time goes in v2:
time: 22.3 us; the launch traced here: 22.2 us
  Pallas kernels  18.8 us (84%)
  local copies, waits for them, and re-layouts  2.7 us (12%)
  between operations  0.66 us (3%)
    pallas_call x1, Pallas kernels, per_device(): pl.pallas_call(functools.partial(kernel, n_r, n_x), out_shape=(out, out),...  18.8 us
    unnamed x8, local copies, waits for them, and re-layouts  2.7 us

profile of v2, /device:TPU:0, one launch (start us, length us, event | category | flops | bytes accessed | tf_op | source)
XLA Modules:
  0.0 22.2 jit_solution(1513544795405079523)
XLA Ops:
  0.6 0.0 copy-start.1
  0.6 0.0 copy-start.2
  0.6 0.6 %copy-done.1 = bf16[96]{0:T(256)(128)(2,1)S(1)} copy-done((bf16[96]{0:T(256)(128)(2,1)S(1)}, bf16[96]{0:T(256)(128)(2,1)}, u32[]{:S(2)}) %copy-start.1) | copy-done | bytes 216
  1.3 0.0 copy-done.2
  1.3 0.0 copy-start
  1.3 0.8 %copy-done = bf16[96,256]{1,0:T(8,128)(2,1)S(1)} copy-done((bf16[96,256]{1,0:T(8,128)(2,1)S(1)}, bf16[96,256]{1,0:T(8,128)(2,1)}, u32[]{:S(2)}) %copy-start) | copy-done | bytes 49176
  2.1 18.8 %shard_map.50 = (bf16[96,256]{1,0:T(8,128)(2,1)S(1)}, bf16[96,256]{1,0:T(8,128)(2,1)S(1)}) custom-call(bf16[96,256]{1,0:T(8,128)(2,1)S(1)} %copy-done, bf16[1,96]{1,0:T(2,128)(2,1)S(1)} %bitcast.2, s32[1,96]{1,0:T(1,128)S(1)} %bitcast.3), custom_call_target="tpu_custom_call" | custom-call | tf_op jit(solution)/shard_map/pallas_call | solution.py:188
  20.9 0.6 %copy.7 = bf16[96,256]{1,0:T(8,128)(2,1)} copy(bf16[96,256]{1,0:T(8,128)(2,1)S(1)} %get-tuple-element.4) | data formatting | bytes 98304
  21.5 0.6 %copy.8 = bf16[96,256]{1,0:T(8,128)(2,1)} copy(bf16[96,256]{1,0:T(8,128)(2,1)S(1)} %get-tuple-element.5) | data formatting | bytes 98304
Async XLA Ops:
  0.6 0.7 %copy-start.1 = (bf16[96]{0:T(256)(128)(2,1)S(1)}, bf16[96]{0:T(256)(128)(2,1)}, u32[]{:S(2)}) copy-start(bf16[96]{0:T(256)(128)(2,1)} %param.4) | copy-start | bytes 580
  0.6 0.7 %copy-start.2 = (s32[96]{0:T(128)S(1)}, s32[96]{0:T(128)}, u32[]{:S(2)}) copy-start(s32[96]{0:T(128)} %param.5) | copy-start | bytes 1156
  1.3 0.8 %copy-start = (bf16[96,256]{1,0:T(8,128)(2,1)S(1)}, bf16[96,256]{1,0:T(8,128)(2,1)}, u32[]{:S(2)}) copy-start(bf16[96,256]{1,0:T(8,128)(2,1)} %emb_hbm.1) | copy-start | bytes 147460

commit v3 on v2

--- a/solution.py
+++ b/solution.py
@@ -15,8 +15,8 @@
 
 
 def kernel(
-    n_r, n_x, emb_hbm, lim_hbm, val_hbm, row_ref, part_ref,
-    buf, emb_ref, lim_ref, val_ref, send, send_c, recv, load,
+    n_r, n_x, emb_hbm, lim_hbm, val_hbm, mix_ref,
+    buf, emb_ref, lim_ref, val_ref, send_z, send_x, send_c, recv, load,
 ):
     rows, width = emb_ref.shape
     cols = width // LANES
@@ -34,7 +34,14 @@
         one.start()
 
     def plane(p):
-        return lax.rem(z + p, n_r)
+        if not few or n_r & (n_r - 1):
+            return lax.rem(z + p, n_r)
+        at, bit = z, 1
+        while bit < n_r:
+            if p & bit:
+                at = at + bit - 2 * bit * lax.rem(z // bit, 2)
+            bit *= 2
+        return at
 
     def column(k):
         return lax.rem(x + k, n_x)
@@ -53,12 +60,24 @@
         else:
             lax.fori_loop(first, last, body, 0)
 
+    def each_x(do):
+        def body(k, carry):
+            do(k)
+            return carry
+
+        if few:
+            for k in range(1, n_x):
+                do(k)
+        else:
+            lax.fori_loop(1, n_x, body, 0)
+
     barrier = pltpu.get_barrier_semaphore()
 
     def greet(z_to, x_to, core_to):
         pl.semaphore_signal(barrier, inc=1, device_id=device(z_to, x_to, core_to), device_id_type=MESH)
 
-    each(1, n_r * n_x, lambda p, k: greet(plane(p), column(k), core))
+    each(1, n_r, lambda p, k: greet(plane(p), x, core))
+    each_x(lambda k: greet(z, column(k), core))
     greet(z, x, 1 - core)
 
     for one in loads:
@@ -77,7 +96,7 @@
     lim_col = jnp.sum(jnp.where(eye, lim_row, 0.0), axis=1, keepdims=True)
     val_col = jnp.sum(jnp.where(eye, val_row.astype(jnp.float32), 0.0), axis=1, keepdims=True)
 
-    pl.semaphore_wait(barrier, n_r * n_x)
+    pl.semaphore_wait(barrier, n_r + n_x - 1)
 
     def copy(z_of, x_of, core_of, sem, to):
         return pltpu.make_async_remote_copy(
@@ -89,8 +108,11 @@
             device_id_type=MESH,
         )
 
-    def out(p, k):
-        return copy(z, x, core, send.at[p, k], device(plane(p), column(k), core))
+    def out(p):
+        return copy(z, x, core, send_z.at[p], device(plane(p), x, core))
+
+    def along(p, k):
+        return copy(plane(p), x, core, send_x.at[p, k], device(z, column(k), core))
 
     def over(p, k):
         return copy(plane(p), column(k), core, send_c.at[p, k], device(z, x, 1 - core))
@@ -99,23 +121,32 @@
         copy(plane(p), column(k), core_of, send_c.at[0, 0], device(z, x, 1 - core)).wait_recv()
 
     if few:
-        order = [(p, k) for k in reversed(range(n_x)) for p in range(n_r) if p or k]
-        for p, k in order:
-            out(p, k).start()
+        near = [1] if n_r > 1 else []
+        for p in [*range(2, n_r), *near]:
+            out(p).start()
     else:
-        each(1, n_r * n_x, lambda p, k: out(p, k).start())
+        each(1, n_r, lambda p, k: out(p).start())
+    each_x(lambda k: along(0, k).start())
     over(0, 0).start()
 
-    def pass_on(p, k):
-        arrived(p, k, core)
-        over(p, k).start()
-
-    def add(planes, k, carry):
+    def from_plane(p, k=0):
+        arrived(p, 0, core)
+        each_x(lambda to: along(p, to).start())
+        over(p, 0).start()
+
+    def from_column(p):
+        def one(k):
+            arrived(p, k, core)
+            over(p, k).start()
+
+        each_x(one)
+
+    def add(pieces, carry):
         sums, row_total, part_total = carry
         others = jnp.concatenate(
             [
                 jnp.concatenate(
-                    [buf[plane(p), column(k), :, c * rows:(c + 1) * rows, :].reshape(2 * rows, LANES) for p in planes],
+                    [buf[plane(p), column(k), :, c * rows:(c + 1) * rows, :].reshape(2 * rows, LANES) for p, k in pieces],
                     axis=0,
                 )
                 for c in range(cols)
@@ -128,7 +159,7 @@
         far = jnp.concatenate(
             [
                 buf[plane(p), column(k), j, cols * rows:, :].astype(jnp.float32)[:1, :rows]
-                for p in planes
+                for p, k in pieces
                 for j in range(2)
             ],
             axis=1,
@@ -148,62 +179,71 @@
         jnp.zeros((rows, 1), jnp.float32),
     )
     if few:
+        last = n_r - 1
+        own = [(p, 0) for p in range(n_r)]
+        early = [(p, k) for k in range(1, n_x) for p in range(last)]
+        late = [(last, k) for k in range(1, n_x)]
+
+        def settle(pieces, carry):
+            for p, k in pieces:
+                arrived(p, k, 1 - core)
+            return add(pieces, carry) if pieces else carry
+
         for p in range(1, n_r):
-            pass_on(p, 0)
-        for p in range(n_r):
-            arrived(p, 0, 1 - core)
-        carry = add(range(n_r), 0, carry)
-        half = (n_r + 1) // 2
-        for k in range(1, n_x):
-            for p in range(n_r):
-                pass_on(p, k)
-            for planes in (range(half), range(half, n_r)):
-                for p in planes:
-                    arrived(p, k, 1 - core)
-                carry = add(planes, k, carry)
+            from_plane(p)
+            if p < last:
+                from_column(p - 1)
+        if n_r > 1:
+            from_column(last - 1)
+        carry = settle(own, carry)
+        from_column(last)
+        carry = settle(early, carry)
+        carry = settle(late, carry)
     else:
-        each(1, n_r * n_x, pass_on)
+        each(1, n_r, from_plane)
+        each(0, n_r, lambda p, k: from_column(p))
         each(0, n_r * n_x, lambda p, k: arrived(p, k, 1 - core))
 
         def step(i, carry):
-            return add((lax.rem(i, n_r),), i // n_r, carry)
+            return add(((lax.rem(i, n_r), i // n_r),), carry)
 
         carry = lax.fori_loop(0, n_r * n_x, step, carry)
     sums, row_total, part_total = carry
 
     scale = width**0.5 * val_col
-    row_ref[...] = (sums[:rows] * (scale / (1.0 + row_total))).astype(jnp.bfloat16)
-    part_ref[...] = (sums[rows:] * (scale / (1.0 + part_total))).astype(jnp.bfloat16)
-
-    each(1, n_r * n_x, lambda p, k: out(p, k).wait_send())
+    mix_ref[:rows, :] = (sums[:rows] * (scale / (1.0 + row_total))).astype(jnp.bfloat16)
+    mix_ref[rows:, :] = (sums[rows:] * (scale / (1.0 + part_total))).astype(jnp.bfloat16)
+
+    each(1, n_r, lambda p, k: out(p).wait_send())
+    each(0, n_r, lambda p, k: each_x(lambda to: along(p, to).wait_send()))
     each(0, n_r * n_x, lambda p, k: over(p, k).wait_send())
 
 
 def per_device(n_r, n_x, embeddings, thresholds, valid):
     rows, width = embeddings.shape
     hbm = pl.BlockSpec(memory_space=pltpu.HBM)
-    vmem = pl.BlockSpec(memory_space=pltpu.VMEM)
-    out = jax.ShapeDtypeStruct((rows, width), jnp.bfloat16)
     shard = (width // LANES) * rows + EXTRA
-    return pl.pallas_call(
+    mix = pl.pallas_call(
         functools.partial(kernel, n_r, n_x),
-        out_shape=(out, out),
+        out_shape=jax.ShapeDtypeStruct((2 * rows, width), jnp.bfloat16),
         in_specs=[hbm] * 3,
-        out_specs=(vmem, vmem),
+        out_specs=pl.BlockSpec(memory_space=pltpu.VMEM),
         scratch_shapes=[
             pltpu.VMEM((n_r, n_x, 2, shard, LANES), jnp.bfloat16),
             pltpu.VMEM((rows, width), embeddings.dtype),
             pltpu.VMEM((1, rows), thresholds.dtype),
             pltpu.VMEM((1, rows), valid.dtype),
+            pltpu.SemaphoreType.DMA((n_r,)),
             pltpu.SemaphoreType.DMA((n_r, n_x)),
             pltpu.SemaphoreType.DMA((n_r, n_x)),
             pltpu.SemaphoreType.DMA((n_r, n_x, 2)),
             pltpu.SemaphoreType.DMA((3,)),
         ],
         compiler_params=pltpu.CompilerParams(
-            collective_id=0, has_side_effects=True, vmem_limit_bytes=48 * 1024 * 1024
+            collective_id=0, has_side_effects=True, vmem_limit_bytes=60 * 1024 * 1024
         ),
     )(embeddings, thresholds.reshape(1, rows), valid.reshape(1, rows))
+    return mix[:rows], mix[rows:]
 
 
 def solution(mesh):

time: 22.3 us -> 19.8 us (0.89)
  the two profiles are of different devices: /device:TPU:0 before, /device:TPU:11 now
where the time goes in v3:
time: 19.8 us; the launch traced here: 19.6 us
  Pallas kernels  17.5 us (88%)
  local copies, waits for them, and re-layouts  1.46 us (7%)
  between operations  0.64 us (3%)
    pallas_call x1, Pallas kernels, per_device(): pl.pallas_call(functools.partial(kernel, n_r, n_x), out_shape=jax.ShapeDt...  17.5 us
    slice x1, local copies, waits for them, and re-layouts, per_device(): return (mix[:rows], mix[rows:])  1.46 us

profile of v3, /device:TPU:11, one launch (start us, length us, event | category | flops | bytes accessed | tf_op | source)
XLA Modules:
  0.0 19.6 jit_solution(3129705726514769612)
XLA Ops:
  0.6 17.5 %shard_map.50 = bf16[192,256]{1,0:T(8,128)(2,1)} custom-call(bf16[96,256]{1,0:T(8,128)(2,1)} %emb_hbm.1, bf16[1,96]{1,0:T(2,128)(2,1)} %bitcast.2, s32[1,96]{1,0:T(1,128)} %bitcast.3), custom_call_target="tpu_custom_call" | custom-call | tf_op jit(solution)/shard_map/pallas_call | solution.py:226
  18.1 1.5 %fusion = (bf16[96,256]{1,0:T(8,128)(2,1)}, bf16[96,256]{1,0:T(8,128)(2,1)}) fusion(bf16[192,256]{1,0:T(8,128)(2,1)} %shard_map.50), kind=kLoop, calls=%fused_computation | loop fusion | bytes 196608 | tf_op jit(solution)/shard_map/slice | solution.py:246

commit v4 on v3

--- a/solution.py
+++ b/solution.py
@@ -24,7 +24,7 @@
     g = lax.axis_index("gc")
     core = lax.rem(g, 2)
     x = g // 2
-    few = n_r * n_x <= 8
+    few = n_x == 2 and n_r <= 4
 
     loads = [
         pltpu.make_async_copy(src, dst, load.at[i])
@@ -77,6 +77,8 @@
         pl.semaphore_signal(barrier, inc=1, device_id=device(z_to, x_to, core_to), device_id_type=MESH)
 
     each(1, n_r, lambda p, k: greet(plane(p), x, core))
+    if few:
+        greet(plane(1), column(1), core)
     each_x(lambda k: greet(z, column(k), core))
     greet(z, x, 1 - core)
 
@@ -96,7 +98,7 @@
     lim_col = jnp.sum(jnp.where(eye, lim_row, 0.0), axis=1, keepdims=True)
     val_col = jnp.sum(jnp.where(eye, val_row.astype(jnp.float32), 0.0), axis=1, keepdims=True)
 
-    pl.semaphore_wait(barrier, n_r + n_x - 1)
+    pl.semaphore_wait(barrier, n_r + n_x - (0 if few else 1))
 
     def copy(z_of, x_of, core_of, sem, to):
         return pltpu.make_async_remote_copy(
@@ -117,21 +119,27 @@
     def over(p, k):
         return copy(plane(p), column(k), core, send_c.at[p, k], device(z, x, 1 - core))
 
+    def diag():
+        return copy(z, x, core, send_x.at[1, 1], device(plane(1), column(1), core))
+
     def arrived(p, k, core_of):
         copy(plane(p), column(k), core_of, send_c.at[0, 0], device(z, x, 1 - core)).wait_recv()
 
     if few:
         near = [1] if n_r > 1 else []
-        for p in [*range(2, n_r), *near]:
+        for p in [*near, *range(2, n_r)]:
             out(p).start()
     else:
         each(1, n_r, lambda p, k: out(p).start())
     each_x(lambda k: along(0, k).start())
+    if few:
+        diag().start()
     over(0, 0).start()
 
     def from_plane(p, k=0):
         arrived(p, 0, core)
-        each_x(lambda to: along(p, to).start())
+        if not few or p != 1:
+            each_x(lambda to: along(p, to).start())
         over(p, 0).start()
 
     def from_column(p):
@@ -225,7 +233,7 @@
     shard = (width // LANES) * rows + EXTRA
     mix = pl.pallas_call(
         functools.partial(kernel, n_r, n_x),
-        out_shape=jax.ShapeDtypeStruct((2 * rows, width), jnp.bfloat16),
+        out_shape=pltpu.VMEM((2 * rows, width), jnp.bfloat16),
         in_specs=[hbm] * 3,
         out_specs=pl.BlockSpec(memory_space=pltpu.VMEM),
         scratch_shapes=[

time: 19.8 us -> 17.2 us (0.87)
  the two profiles are of different devices: /device:TPU:11 before, /device:TPU:1 now
where the time goes in v4:
time: 17.2 us; the launch traced here: 17.1 us
  Pallas kernels  15.8 us (92%)
  local copies, waits for them, and re-layouts  0.64 us (4%)
  between operations  0.64 us (4%)
    pallas_call x1, Pallas kernels, per_device(): pl.pallas_call(functools.partial(kernel, n_r, n_x), out_shape=pltpu.VMEM(...  15.8 us
    slice x1, local copies, waits for them, and re-layouts, per_device(): return (mix[:rows], mix[rows:])  0.64 us

profile of v4, /device:TPU:1, one launch (start us, length us, event | category | flops | bytes accessed | tf_op | source)
XLA Modules:
  0.0 17.1 jit_solution(8916377933520772798)
XLA Ops:
  0.6 15.8 %shard_map.50 = bf16[192,256]{1,0:T(8,128)(2,1)S(1)} custom-call(bf16[96,256]{1,0:T(8,128)(2,1)} %emb_hbm.1, bf16[1,96]{1,0:T(2,128)(2,1)} %bitcast.2, s32[1,96]{1,0:T(1,128)} %bitcast.3), custom_call_target="tpu_custom_call" | custom-call | tf_op jit(solution)/shard_map/pallas_call | solution.py:234
  16.4 0.6 %fusion = (bf16[96,256]{1,0:T(8,128)(2,1)}, bf16[96,256]{1,0:T(8,128)(2,1)}) fusion(bf16[192,256]{1,0:T(8,128)(2,1)S(1)} %shard_map.50), kind=kLoop, calls=%fused_computation | loop fusion | bytes 196608 | tf_op jit(solution)/shard_map/slice | solution.py:254

commit v5 on v4

--- a/solution.py
+++ b/solution.py
@@ -94,10 +94,6 @@
     far_pad = jnp.concatenate([far_row, jnp.full((1, LANES - rows), FAR, jnp.float32)], axis=1)
     buf[z, x, core, cols * rows:, :] = jnp.broadcast_to(far_pad, (EXTRA, LANES)).astype(jnp.bfloat16)
 
-    eye = lax.broadcasted_iota(jnp.int32, (rows, rows), 0) == lax.broadcasted_iota(jnp.int32, (rows, rows), 1)
-    lim_col = jnp.sum(jnp.where(eye, lim_row, 0.0), axis=1, keepdims=True)
-    val_col = jnp.sum(jnp.where(eye, val_row.astype(jnp.float32), 0.0), axis=1, keepdims=True)
-
     pl.semaphore_wait(barrier, n_r + n_x - (0 if few else 1))
 
     def copy(z_of, x_of, core_of, sem, to):
@@ -131,10 +127,14 @@
             out(p).start()
     else:
         each(1, n_r, lambda p, k: out(p).start())
+    if few:
+        diag().start()
     each_x(lambda k: along(0, k).start())
-    if few:
-        diag().start()
     over(0, 0).start()
+
+    eye = lax.broadcasted_iota(jnp.int32, (rows, rows), 0) == lax.broadcasted_iota(jnp.int32, (rows, rows), 1)
+    lim_col = jnp.sum(jnp.where(eye, lim_row, 0.0), axis=1, keepdims=True)
+    val_col = jnp.sum(jnp.where(eye, val_row.astype(jnp.float32), 0.0), axis=1, keepdims=True)
 
     def from_plane(p, k=0):
         arrived(p, 0, core)

time: 17.2 us -> 17.2 us (level)
  no operation moved by 1% of the time
where the time goes in v5:
time: 17.2 us; the launch traced here: 17 us
  Pallas kernels  15.8 us (92%)
  local copies, waits for them, and re-layouts  0.64 us (4%)
  between operations  0.64 us (4%)
    pallas_call x1, Pallas kernels, per_device(): pl.pallas_call(functools.partial(kernel, n_r, n_x), out_shape=pltpu.VMEM(...  15.8 us
    slice x1, local copies, waits for them, and re-layouts, per_device(): return (mix[:rows], mix[rows:])  0.64 us

profile of v5, /device:TPU:1, one launch (start us, length us, event | category | flops | bytes accessed | tf_op | source)
XLA Modules:
  0.0 17.0 jit_solution(1314041308037947181)
XLA Ops:
  0.6 15.8 %shard_map.50 = bf16[192,256]{1,0:T(8,128)(2,1)S(1)} custom-call(bf16[96,256]{1,0:T(8,128)(2,1)} %emb_hbm.1, bf16[1,96]{1,0:T(2,128)(2,1)} %bitcast.2, s32[1,96]{1,0:T(1,128)} %bitcast.3), custom_call_target="tpu_custom_call" | custom-call | tf_op jit(solution)/shard_map/pallas_call | solution.py:234
  16.4 0.6 %fusion = (bf16[96,256]{1,0:T(8,128)(2,1)}, bf16[96,256]{1,0:T(8,128)(2,1)}) fusion(bf16[192,256]{1,0:T(8,128)(2,1)S(1)} %shard_map.50), kind=kLoop, calls=%fused_computation | loop fusion | bytes 196608 | tf_op jit(solution)/shard_map/slice | solution.py:254
